TPU v7x, 32 devices: a whole 2x2x4 slice. The times are simulated.
32 devices in a mesh: dp: 32 (over z, y, x, core).
Axes of the slice: x: 2, y: 2, z: 4, core: 2. Of those that a mesh axis runs over, the one named last changes fastest.
Arguments:
- picture_embeddings_raw: float32 [8192, 1152], P('dp'), may hold values from -0.18 to 0.18
- caption_embeddings_raw: float32 [8192, 1152], P('dp'), may hold values from -0.18 to 0.18
- sharpness_array: float32 [1], replicated, may hold values from 5 to 15
- offset_term_array: float32 [1], replicated, may hold values from -4 to -1
Outputs:
- row_loss: float32 [8192], P('dp')
- grad_image: float32 [8192, 1152], P('dp')
- grad_text: float32 [8192, 1152], P('dp')
All inputs are finite; a program needn't handle non-finite values.
Results may differ from a plain program's by a relative error of at most 0.003.
Values may be sent and summed in bfloat16 or wider, within the bound.
A program may use at most 64 MiB of HBM per device.

v0:
```python
import jax
import jax.numpy as jnp
from jax import lax
from jax.sharding import PartitionSpec as P

STEPS = 8


epsilon = 1e-06


def shifted(value, axis, by):
    size = lax.axis_size(axis)
    return lax.ppermute(value, axis, [(i, (i + by) % size) for i in range(size)])


def unit_rows(values):
    radius = jnp.sqrt(jnp.sum(values * values, axis=-1, keepdims=True) + epsilon)
    return (values / radius, radius)


def back_rows(grad_unit, unit, radius):
    inner = jnp.sum(unit * grad_unit, axis=-1, keepdims=True)
    return (grad_unit - unit * inner) / radius


def per_device(picture_embeddings_raw, caption_embeddings_raw, sharpness_array, offset_term_array):
    row_count = picture_embeddings_raw.shape[0]
    step_total = STEPS
    half_steps = step_total // 2
    image_unit_vectors, img_radius = unit_rows(picture_embeddings_raw)
    txt_unit, txt_radius = unit_rows(caption_embeddings_raw)
    txt_send = txt_unit.astype(jnp.bfloat16)
    sharpness_multiplier = sharpness_array[0]
    additive_offset_term = offset_term_array[0]
    diagonal_ones = jnp.eye(row_count, dtype=jnp.float32)

    def labels(offset):
        if offset == 0:
            return diagonal_ones
        return jnp.zeros_like(diagonal_ones)

    chains = (-half_steps, 1, step_total)
    loss_total = jnp.zeros((row_count,), jnp.float32)
    picture_derivative_sum = jnp.zeros_like(image_unit_vectors)
    first_offset, direction, chain_steps = chains
    text_block = shifted(txt_send, "dp", -first_offset)
    carried = jnp.zeros_like(txt_unit)
    offset = first_offset
    for turn_index in range(chain_steps):
        offset = first_offset + direction * turn_index
        if turn_index > 0:
            text_block = shifted(text_block, "dp", -direction)
            carried = shifted(carried, "dp", -direction)
        neighbor_shard_index = text_block.astype(jnp.float32)
        matching_scores = (
            sharpness_multiplier
            * jnp.dot(image_unit_vectors, neighbor_shard_index.T, precision=lax.Precision.HIGHEST)
            + additive_offset_term
        )
        positive = labels(offset)
        loss_rows = jnp.sum(jax.nn.softplus(matching_scores) - positive * matching_scores, axis=1)
        match_weight_factor = jax.nn.sigmoid(matching_scores) - positive
        picture_piece = sharpness_multiplier * jnp.dot(
            match_weight_factor, neighbor_shard_index, precision=lax.Precision.HIGHEST
        )
        caption_piece = sharpness_multiplier * jnp.dot(
            match_weight_factor.T, image_unit_vectors, precision=lax.Precision.HIGHEST
        )
        loss_rows, picture_piece, caption_piece = (loss_rows, picture_piece, caption_piece)
        loss_total = loss_total + loss_rows
        picture_derivative_sum = picture_derivative_sum + picture_piece
        carried = carried + caption_piece
    text_total = shifted(carried, "dp", offset)
    row_loss = loss_total / (step_total * row_count)
    grad_image = back_rows(picture_derivative_sum, image_unit_vectors, img_radius)
    grad_text = back_rows(text_total, txt_unit, txt_radius)
    return (row_loss, grad_image, grad_text)


def solution(mesh):
    return jax.shard_map(
        per_device,
        mesh=mesh,
        in_specs=(P("dp", None), P("dp", None), P(), P()),
        out_specs=(P("dp"), P("dp", None), P("dp", None)),
        check_vma=False,
    )
```

profile of v0, /device:TPU:0, one launch (start us, length us, event | category | flops | bytes accessed | tf_op | source)
XLA Modules:
  0.0 196.7 jit_solution(5476516916915776323)
XLA Ops:
  0.6 1.5 multiply_reduce_fusion.2
  2.4 3.0 %collective-permute-start = (bf16[256,1152]{1,0:T(8,128)(2,1)S(1)}, bf16[256,1152]{1,0:T(8,128)(2,1)S(1)}, u32[]{:S(2)}, u32[]{:S(2)}) collective-permute-start(bf16[256,1152]{1,0:T(8,128)(2,1)S(1)} %fusion.43), channel_id=1, source_target_pairs={{0,4},{1,5},{2,6},{3,7},{4,8},{5,9},{6,10},{7,11},{8,12},{9,13},{1... | collective-permute-start | bytes 1769480 | tf_op jit(solution)/shard_map/ppermute | solution.py:14
  6.9 14.9 %collective-permute-done = bf16[256,1152]{1,0:T(8,128)(2,1)S(1)} collective-permute-done((bf16[256,1152]{1,0:T(8,128)(2,1)S(1)}, bf16[256,1152]{1,0:T(8,128)(2,1)S(1)}, u32[]{:S(2)}, u32[]{:S(2)}) %collective-permute-start) | collective-permute-done | bytes 589856 | tf_op jit(solution)/shard_map/ppermute | solution.py:14
  25.6 1.5 collective-permute-start.1
  27.2 18.5 %collective-permute-done.1 = bf16[256,1152]{1,0:T(8,128)(2,1)S(1)} collective-permute-done((bf16[256,1152]{1,0:T(8,128)(2,1)S(1)}, bf16[256,1152]{1,0:T(8,128)(2,1)S(1)}, u32[]{:S(2)}, u32[]{:S(2)}) %collective-permute-start.1) | collective-permute-done | bytes 589856 | tf_op jit(solution)/shard_map/ppermute | solution.py:14
  45.7 5.5 %collective-permute-start.2 = (bf16[256,1152]{1,0:T(8,128)(2,1)S(1)}, bf16[256,1152]{1,0:T(8,128)(2,1)S(1)}, u32[]{:S(2)}, u32[]{:S(2)}) collective-permute-start(bf16[256,1152]{1,0:T(8,128)(2,1)S(1)} %collective-permute-done.1), channel_id=1, source_target_pairs={{0,31},{1,0},{2,1},{3,2},{4,3},{5,4},{6,5},{7,6},{8,7},{9,8},{10,9... | collective-permute-start | bytes 1769480 | tf_op jit(solution)/shard_map/ppermute | solution.py:14
  53.8 4.8 %collective-permute-done.2 = bf16[256,1152]{1,0:T(8,128)(2,1)S(1)} collective-permute-done((bf16[256,1152]{1,0:T(8,128)(2,1)S(1)}, bf16[256,1152]{1,0:T(8,128)(2,1)S(1)}, u32[]{:S(2)}, u32[]{:S(2)}) %collective-permute-start.2) | collective-permute-done | bytes 589856 | tf_op jit(solution)/shard_map/ppermute | solution.py:14
  58.6 5.5 %collective-permute-start.3 = (bf16[256,1152]{1,0:T(8,128)(2,1)S(1)}, bf16[256,1152]{1,0:T(8,128)(2,1)S(1)}, u32[]{:S(2)}, u32[]{:S(2)}) collective-permute-start(bf16[256,1152]{1,0:T(8,128)(2,1)S(1)} %collective-permute-done.2), channel_id=1, source_target_pairs={{0,31},{1,0},{2,1},{3,2},{4,3},{5,4},{6,5},{7,6},{8,7},{9,8},{10,9... | collective-permute-start | bytes 1769480 | tf_op jit(solution)/shard_map/ppermute | solution.py:14
  66.6 4.6 %collective-permute-done.9 = f32[256,1152]{1,0:T(8,128)S(1)} collective-permute-done((f32[256,1152]{1,0:T(8,128)S(1)}, f32[256,1152]{1,0:T(8,128)S(1)}, u32[]{:S(2)}, u32[]{:S(2)}) %collective-permute-start.9) | collective-permute-done | bytes 1179680 | tf_op jit(solution)/shard_map/ppermute | solution.py:14
  71.3 5.6 %collective-permute-start.10 = (f32[256,1152]{1,0:T(8,128)S(1)}, f32[256,1152]{1,0:T(8,128)S(1)}, u32[]{:S(2)}, u32[]{:S(2)}) collective-permute-start(f32[256,1152]{1,0:T(8,128)S(1)} %add.204), channel_id=1, source_target_pairs={{0,31},{1,0},{2,1},{3,2},{4,3},{5,4},{6,5},{7,6},{8,7},{9,8},{10,9... | collective-permute-start | bytes 3538952 | tf_op jit(solution)/shard_map/ppermute | solution.py:14
  77.5 5.5 %collective-permute-start.4 = (bf16[256,1152]{1,0:T(8,128)(2,1)S(1)}, bf16[256,1152]{1,0:T(8,128)(2,1)S(1)}, u32[]{:S(2)}, u32[]{:S(2)}) collective-permute-start(bf16[256,1152]{1,0:T(8,128)(2,1)S(1)} %collective-permute-done.3), channel_id=1, source_target_pairs={{0,31},{1,0},{2,1},{3,2},{4,3},{5,4},{6,5},{7,6},{8,7},{9,8},{10,9... | collective-permute-start | bytes 1769480 | tf_op jit(solution)/shard_map/ppermute | solution.py:14
  85.6 5.0 %collective-permute-done.10 = f32[256,1152]{1,0:T(8,128)S(1)} collective-permute-done((f32[256,1152]{1,0:T(8,128)S(1)}, f32[256,1152]{1,0:T(8,128)S(1)}, u32[]{:S(2)}, u32[]{:S(2)}) %collective-permute-start.10) | collective-permute-done | bytes 1179680 | tf_op jit(solution)/shard_map/ppermute | solution.py:14
  90.7 5.6 %collective-permute-start.11 = (f32[256,1152]{1,0:T(8,128)S(1)}, f32[256,1152]{1,0:T(8,128)S(1)}, u32[]{:S(2)}, u32[]{:S(2)}) collective-permute-start(f32[256,1152]{1,0:T(8,128)S(1)} %add.205), channel_id=1, source_target_pairs={{0,31},{1,0},{2,1},{3,2},{4,3},{5,4},{6,5},{7,6},{8,7},{9,8},{10,9... | collective-permute-start | bytes 3538952 | tf_op jit(solution)/shard_map/ppermute | solution.py:14
  97.1 5.4 %collective-permute-start.5 = (bf16[256,1152]{1,0:T(8,128)(2,1)S(1)}, bf16[256,1152]{1,0:T(8,128)(2,1)S(1)}, u32[]{:S(2)}, u32[]{:S(2)}) collective-permute-start(bf16[256,1152]{1,0:T(8,128)(2,1)S(1)} %collective-permute-done.4), channel_id=1, source_target_pairs={{0,31},{1,0},{2,1},{3,2},{4,3},{5,4},{6,5},{7,6},{8,7},{9,8},{10,9... | collective-permute-start | bytes 1769480 | tf_op jit(solution)/shard_map/ppermute | solution.py:14
  105.0 5.0 %collective-permute-done.11 = f32[256,1152]{1,0:T(8,128)S(1)} collective-permute-done((f32[256,1152]{1,0:T(8,128)S(1)}, f32[256,1152]{1,0:T(8,128)S(1)}, u32[]{:S(2)}, u32[]{:S(2)}) %collective-permute-start.11) | collective-permute-done | bytes 1179680 | tf_op jit(solution)/shard_map/ppermute | solution.py:14
  110.1 5.6 %collective-permute-start.12 = (f32[256,1152]{1,0:T(8,128)S(1)}, f32[256,1152]{1,0:T(8,128)S(1)}, u32[]{:S(2)}, u32[]{:S(2)}) collective-permute-start(f32[256,1152]{1,0:T(8,128)S(1)} %add.206), channel_id=1, source_target_pairs={{0,31},{1,0},{2,1},{3,2},{4,3},{5,4},{6,5},{7,6},{8,7},{9,8},{10,9... | collective-permute-start | bytes 3538952 | tf_op jit(solution)/shard_map/ppermute | solution.py:14
  117.3 4.5 %collective-permute-start.6 = (bf16[256,1152]{1,0:T(8,128)(2,1)S(1)}, bf16[256,1152]{1,0:T(8,128)(2,1)S(1)}, u32[]{:S(2)}, u32[]{:S(2)}) collective-permute-start(bf16[256,1152]{1,0:T(8,128)(2,1)S(1)} %collective-permute-done.5), channel_id=1, source_target_pairs={{0,31},{1,0},{2,1},{3,2},{4,3},{5,4},{6,5},{7,6},{8,7},{9,8},{10,9... | collective-permute-start | bytes 1769480 | tf_op jit(solution)/shard_map/ppermute | solution.py:14
  124.4 5.0 %collective-permute-done.12 = f32[256,1152]{1,0:T(8,128)S(1)} collective-permute-done((f32[256,1152]{1,0:T(8,128)S(1)}, f32[256,1152]{1,0:T(8,128)S(1)}, u32[]{:S(2)}, u32[]{:S(2)}) %collective-permute-start.12) | collective-permute-done | bytes 1179680 | tf_op jit(solution)/shard_map/ppermute | solution.py:14
  129.5 5.6 %collective-permute-start.13 = (f32[256,1152]{1,0:T(8,128)S(1)}, f32[256,1152]{1,0:T(8,128)S(1)}, u32[]{:S(2)}, u32[]{:S(2)}) collective-permute-start(f32[256,1152]{1,0:T(8,128)S(1)} %add.207), channel_id=1, source_target_pairs={{0,31},{1,0},{2,1},{3,2},{4,3},{5,4},{6,5},{7,6},{8,7},{9,8},{10,9... | collective-permute-start | bytes 3538952 | tf_op jit(solution)/shard_map/ppermute | solution.py:14
  136.7 4.5 %collective-permute-start.7 = (bf16[256,1152]{1,0:T(8,128)(2,1)S(1)}, bf16[256,1152]{1,0:T(8,128)(2,1)S(1)}, u32[]{:S(2)}, u32[]{:S(2)}) collective-permute-start(bf16[256,1152]{1,0:T(8,128)(2,1)S(1)} %collective-permute-done.6), channel_id=1, source_target_pairs={{0,31},{1,0},{2,1},{3,2},{4,3},{5,4},{6,5},{7,6},{8,7},{9,8},{10,9... | collective-permute-start | bytes 1769480 | tf_op jit(solution)/shard_map/ppermute | solution.py:14
  143.8 5.0 %collective-permute-done.13 = f32[256,1152]{1,0:T(8,128)S(1)} collective-permute-done((f32[256,1152]{1,0:T(8,128)S(1)}, f32[256,1152]{1,0:T(8,128)S(1)}, u32[]{:S(2)}, u32[]{:S(2)}) %collective-permute-start.13) | collective-permute-done | bytes 1179680 | tf_op jit(solution)/shard_map/ppermute | solution.py:14
  148.9 5.8 %collective-permute-start.14 = (f32[256,1152]{1,0:T(8,128)S(1)}, f32[256,1152]{1,0:T(8,128)S(1)}, u32[]{:S(2)}, u32[]{:S(2)}) collective-permute-start(f32[256,1152]{1,0:T(8,128)S(1)} %add.208), channel_id=1, source_target_pairs={{0,31},{1,0},{2,1},{3,2},{4,3},{5,4},{6,5},{7,6},{8,7},{9,8},{10,9... | collective-permute-start | bytes 3538952 | tf_op jit(solution)/shard_map/ppermute | solution.py:14
  158.9 9.6 %collective-permute-done.14 = f32[256,1152]{1,0:T(8,128)S(1)} collective-permute-done((f32[256,1152]{1,0:T(8,128)S(1)}, f32[256,1152]{1,0:T(8,128)S(1)}, u32[]{:S(2)}, u32[]{:S(2)}) %collective-permute-start.14) | collective-permute-done | bytes 1179680 | tf_op jit(solution)/shard_map/ppermute | solution.py:14
  171.5 23.6 %collective-permute-done.15 = f32[256,1152]{1,0:T(8,128)S(1)} collective-permute-done((f32[256,1152]{1,0:T(8,128)S(1)}, f32[256,1152]{1,0:T(8,128)S(1)}, u32[]{:S(2)}, u32[]{:S(2)}) %collective-permute-start.15) | collective-permute-done | bytes 1179680 | tf_op jit(solution)/shard_map/ppermute | solution.py:14
  (51 shorter events, 33.4 us)
Async XLA Ops:
  0.6 1.6 copy-start
  2.2 4.6 %copy-start.1 = (f32[256,1152]{1,0:T(8,128)S(1)}, f32[256,1152]{1,0:T(8,128)}, u32[]{:S(2)}) copy-start(f32[256,1152]{1,0:T(8,128)} %param.4) | copy-start | bytes 3538948
  2.4 19.4 %collective-permute-start = (bf16[256,1152]{1,0:T(8,128)(2,1)S(1)}, bf16[256,1152]{1,0:T(8,128)(2,1)S(1)}, u32[]{:S(2)}, u32[]{:S(2)}) collective-permute-start(bf16[256,1152]{1,0:T(8,128)(2,1)S(1)} %fusion.43), channel_id=1, source_target_pairs={{0,4},{1,5},{2,6},{3,7},{4,8},{5,9},{6,10},{7,11},{8,12},{9,13},{1... | collective-permute-start | bytes 1769480 | tf_op jit(solution)/shard_map/ppermute | solution.py:14
  24.3 28.0 %collective-permute-start.8 = (f32[256,1152]{1,0:T(8,128)S(1)}, f32[256,1152]{1,0:T(8,128)S(1)}, u32[]{:S(2)}, u32[]{:S(2)}) collective-permute-start(f32[256,1152]{1,0:T(8,128)S(1)} %convolution_multiply_fusion.7), channel_id=1, source_target_pairs={{0,31},{1,0},{2,1},{3,2},{4,3},{5,4},{6,5},{7,6},{8,7},{9,8},{10,9... | collective-permute-start | bytes 3538952 | tf_op jit(solution)/shard_map/ppermute | solution.py:14
  25.6 20.0 %collective-permute-start.1 = (bf16[256,1152]{1,0:T(8,128)(2,1)S(1)}, bf16[256,1152]{1,0:T(8,128)(2,1)S(1)}, u32[]{:S(2)}, u32[]{:S(2)}) collective-permute-start(bf16[256,1152]{1,0:T(8,128)(2,1)S(1)} %collective-permute-done), channel_id=1, source_target_pairs={{0,31},{1,0},{2,1},{3,2},{4,3},{5,4},{6,5},{7,6},{8,7},{9,8},{10,9... | collective-permute-start | bytes 1769480 | tf_op jit(solution)/shard_map/ppermute | solution.py:14
  45.7 12.9 %collective-permute-start.2 = (bf16[256,1152]{1,0:T(8,128)(2,1)S(1)}, bf16[256,1152]{1,0:T(8,128)(2,1)S(1)}, u32[]{:S(2)}, u32[]{:S(2)}) collective-permute-start(bf16[256,1152]{1,0:T(8,128)(2,1)S(1)} %collective-permute-done.1), channel_id=1, source_target_pairs={{0,31},{1,0},{2,1},{3,2},{4,3},{5,4},{6,5},{7,6},{8,7},{9,8},{10,9... | collective-permute-start | bytes 1769480 | tf_op jit(solution)/shard_map/ppermute | solution.py:14
  53.7 17.5 %collective-permute-start.9 = (f32[256,1152]{1,0:T(8,128)S(1)}, f32[256,1152]{1,0:T(8,128)S(1)}, u32[]{:S(2)}, u32[]{:S(2)}) collective-permute-start(f32[256,1152]{1,0:T(8,128)S(1)} %fusion.1), channel_id=1, source_target_pairs={{0,31},{1,0},{2,1},{3,2},{4,3},{5,4},{6,5},{7,6},{8,7},{9,8},{10,9... | collective-permute-start | bytes 3538952 | tf_op jit(solution)/shard_map/ppermute | solution.py:14
  58.6 19.0 %collective-permute-start.3 = (bf16[256,1152]{1,0:T(8,128)(2,1)S(1)}, bf16[256,1152]{1,0:T(8,128)(2,1)S(1)}, u32[]{:S(2)}, u32[]{:S(2)}) collective-permute-start(bf16[256,1152]{1,0:T(8,128)(2,1)S(1)} %collective-permute-done.2), channel_id=1, source_target_pairs={{0,31},{1,0},{2,1},{3,2},{4,3},{5,4},{6,5},{7,6},{8,7},{9,8},{10,9... | collective-permute-start | bytes 1769480 | tf_op jit(solution)/shard_map/ppermute | solution.py:14
  71.3 19.3 %collective-permute-start.10 = (f32[256,1152]{1,0:T(8,128)S(1)}, f32[256,1152]{1,0:T(8,128)S(1)}, u32[]{:S(2)}, u32[]{:S(2)}) collective-permute-start(f32[256,1152]{1,0:T(8,128)S(1)} %add.204), channel_id=1, source_target_pairs={{0,31},{1,0},{2,1},{3,2},{4,3},{5,4},{6,5},{7,6},{8,7},{9,8},{10,9... | collective-permute-start | bytes 3538952 | tf_op jit(solution)/shard_map/ppermute | solution.py:14
  77.5 19.5 %collective-permute-start.4 = (bf16[256,1152]{1,0:T(8,128)(2,1)S(1)}, bf16[256,1152]{1,0:T(8,128)(2,1)S(1)}, u32[]{:S(2)}, u32[]{:S(2)}) collective-permute-start(bf16[256,1152]{1,0:T(8,128)(2,1)S(1)} %collective-permute-done.3), channel_id=1, source_target_pairs={{0,31},{1,0},{2,1},{3,2},{4,3},{5,4},{6,5},{7,6},{8,7},{9,8},{10,9... | collective-permute-start | bytes 1769480 | tf_op jit(solution)/shard_map/ppermute | solution.py:14
  90.7 19.3 %collective-permute-start.11 = (f32[256,1152]{1,0:T(8,128)S(1)}, f32[256,1152]{1,0:T(8,128)S(1)}, u32[]{:S(2)}, u32[]{:S(2)}) collective-permute-start(f32[256,1152]{1,0:T(8,128)S(1)} %add.205), channel_id=1, source_target_pairs={{0,31},{1,0},{2,1},{3,2},{4,3},{5,4},{6,5},{7,6},{8,7},{9,8},{10,9... | collective-permute-start | bytes 3538952 | tf_op jit(solution)/shard_map/ppermute | solution.py:14
  97.1 20.2 %collective-permute-start.5 = (bf16[256,1152]{1,0:T(8,128)(2,1)S(1)}, bf16[256,1152]{1,0:T(8,128)(2,1)S(1)}, u32[]{:S(2)}, u32[]{:S(2)}) collective-permute-start(bf16[256,1152]{1,0:T(8,128)(2,1)S(1)} %collective-permute-done.4), channel_id=1, source_target_pairs={{0,31},{1,0},{2,1},{3,2},{4,3},{5,4},{6,5},{7,6},{8,7},{9,8},{10,9... | collective-permute-start | bytes 1769480 | tf_op jit(solution)/shard_map/ppermute | solution.py:14
  110.1 19.3 %collective-permute-start.12 = (f32[256,1152]{1,0:T(8,128)S(1)}, f32[256,1152]{1,0:T(8,128)S(1)}, u32[]{:S(2)}, u32[]{:S(2)}) collective-permute-start(f32[256,1152]{1,0:T(8,128)S(1)} %add.206), channel_id=1, source_target_pairs={{0,31},{1,0},{2,1},{3,2},{4,3},{5,4},{6,5},{7,6},{8,7},{9,8},{10,9... | collective-permute-start | bytes 3538952 | tf_op jit(solution)/shard_map/ppermute | solution.py:14
  117.3 19.4 %collective-permute-start.6 = (bf16[256,1152]{1,0:T(8,128)(2,1)S(1)}, bf16[256,1152]{1,0:T(8,128)(2,1)S(1)}, u32[]{:S(2)}, u32[]{:S(2)}) collective-permute-start(bf16[256,1152]{1,0:T(8,128)(2,1)S(1)} %collective-permute-done.5), channel_id=1, source_target_pairs={{0,31},{1,0},{2,1},{3,2},{4,3},{5,4},{6,5},{7,6},{8,7},{9,8},{10,9... | collective-permute-start | bytes 1769480 | tf_op jit(solution)/shard_map/ppermute | solution.py:14
  129.5 19.3 %collective-permute-start.13 = (f32[256,1152]{1,0:T(8,128)S(1)}, f32[256,1152]{1,0:T(8,128)S(1)}, u32[]{:S(2)}, u32[]{:S(2)}) collective-permute-start(f32[256,1152]{1,0:T(8,128)S(1)} %add.207), channel_id=1, source_target_pairs={{0,31},{1,0},{2,1},{3,2},{4,3},{5,4},{6,5},{7,6},{8,7},{9,8},{10,9... | collective-permute-start | bytes 3538952 | tf_op jit(solution)/shard_map/ppermute | solution.py:14
  136.7 19.6 %collective-permute-start.7 = (bf16[256,1152]{1,0:T(8,128)(2,1)S(1)}, bf16[256,1152]{1,0:T(8,128)(2,1)S(1)}, u32[]{:S(2)}, u32[]{:S(2)}) collective-permute-start(bf16[256,1152]{1,0:T(8,128)(2,1)S(1)} %collective-permute-done.6), channel_id=1, source_target_pairs={{0,31},{1,0},{2,1},{3,2},{4,3},{5,4},{6,5},{7,6},{8,7},{9,8},{10,9... | collective-permute-start | bytes 1769480 | tf_op jit(solution)/shard_map/ppermute | solution.py:14
  148.9 19.5 %collective-permute-start.14 = (f32[256,1152]{1,0:T(8,128)S(1)}, f32[256,1152]{1,0:T(8,128)S(1)}, u32[]{:S(2)}, u32[]{:S(2)}) collective-permute-start(f32[256,1152]{1,0:T(8,128)S(1)} %add.208), channel_id=1, source_target_pairs={{0,31},{1,0},{2,1},{3,2},{4,3},{5,4},{6,5},{7,6},{8,7},{9,8},{10,9... | collective-permute-start | bytes 3538952 | tf_op jit(solution)/shard_map/ppermute | solution.py:14
  168.6 26.6 %collective-permute-start.15 = (f32[256,1152]{1,0:T(8,128)S(1)}, f32[256,1152]{1,0:T(8,128)S(1)}, u32[]{:S(2)}, u32[]{:S(2)}) collective-permute-start(f32[256,1152]{1,0:T(8,128)S(1)} %add.209), channel_id=1, source_target_pairs={{0,3},{1,4},{2,5},{3,6},{4,7},{5,8},{6,9},{7,10},{8,11},{9,12},{10... | collective-permute-start | bytes 3538952 | tf_op jit(solution)/shard_map/ppermute | solution.py:14
where the time goes:
time: 197 us
  waiting for transfers between devices  96.7 us (49%)
  starting transfers between devices  64.9 us (33%)
  matrix products  26.9 us (14%)
  other arithmetic  5.93 us (3%)
  between operations  2.14 us (1%)
    ppermute x16, waiting for transfers between devices, shifted(): lax.ppermute(value, axis, [(i, (i + by) % size) for i in range(size)])  96.7 us
    ppermute x16, starting transfers between devices, shifted(): lax.ppermute(value, axis, [(i, (i + by) % size) for i in range(size)])  64.9 us
    dot_general x8, matrix products, per_device(): jnp.dot(match_weight_factor.T, image_unit_vectors, precision=lax.Precisio...  11.1 us
    dot_general x8, matrix products, per_device(): jnp.dot(image_unit_vectors, neighbor_shard_index.T, precision=lax.Precisi...  9.2 us
    dot_general x8, matrix products, per_device(): jnp.dot(match_weight_factor, neighbor_shard_index, precision=lax.Precisio...  6.57 us
  transfers between devices with their start and end apart: 16, of which 11 were waited for; matrix products, arithmetic and copies ran while one was open for 14% of the time, Pallas kernels for 0%

commit v1 on v0

--- a/solution.py
+++ b/solution.py
@@ -1,6 +1,10 @@
+import functools
+
 import jax
 import jax.numpy as jnp
 from jax import lax
+from jax.experimental import pallas as pl
+from jax.experimental.pallas import tpu as pltpu
 from jax.sharding import PartitionSpec as P
 
 STEPS = 8
@@ -78,9 +82,268 @@
     return (row_loss, grad_image, grad_text)
 
 
+OWN, SIB, X, Y, Z, V, FAR, SIB_X, SIB_E, SIB_F = range(10)
+SLOTS = 10
+CHUNKS = 2
+SENDS = 18
+
+
+def tree_kernel(
+    picture_ref, caption_ref, sharp_ref, offset_ref,
+    loss_ref, grad_image_ref, grad_text_ref,
+    txt, img, img_low, txt_sem, img_sem, send_sem,
+):
+    rows, width = picture_ref.shape
+    part = rows // CHUNKS
+    me = lax.axis_index("dp")
+    total = lax.axis_size("dp")
+    core = lax.rem(me, 2)
+    x = lax.rem(me // 2, 2)
+    y = lax.rem(me // 4, 2)
+    corner = x == y
+    plane = 8
+    to_x = me + 2 - 4 * x
+    to_y = me + 4 - 8 * y
+    to_sib = me + 1 - 2 * core
+    step = plane - 2 * plane * y
+    z_out = lax.rem(me + step + total, total)
+    z_in = lax.rem(me - step + total, total)
+    skip_txt_z = jnp.logical_and(jnp.logical_and(x == 1, y == 1), core == 1)
+    skip_img_z = jnp.logical_and(y == 0, core == 0)
+
+    barrier = pltpu.get_barrier_semaphore()
+    for peer in (to_x, to_y, to_sib, z_in):
+        pl.semaphore_signal(barrier, inc=1, device_id=(peer,), device_id_type=pl.DeviceIdType.MESH)
+
+    def copy(buf, sem, src, dst, chunk, number, target):
+        at = pl.ds(chunk * part, part)
+        return pltpu.make_async_remote_copy(
+            src_ref=buf.at[src, at],
+            dst_ref=buf.at[dst, at],
+            send_sem=send_sem.at[number, chunk],
+            recv_sem=sem.at[dst, chunk],
+            device_id=(target,),
+            device_id_type=pl.DeviceIdType.MESH,
+        )
+
+    def send_txt(src, dst, chunk, number, target):
+        copy(txt, txt_sem, src, dst, chunk, number, target).start()
+
+    def send_img(src, dst, chunk, number, target):
+        copy(img, img_sem, src, dst, chunk, number, target).start()
+
+    def wait_txt(dst, chunk):
+        copy(txt, txt_sem, dst, dst, chunk, 0, to_sib).wait_recv()
+
+    def wait_img(dst, chunk):
+        copy(img, img_sem, dst, dst, chunk, 0, to_sib).wait_recv()
+
+    def unit(values):
+        radius = jnp.sqrt(jnp.sum(values * values, axis=-1, keepdims=True) + epsilon)
+        return values / radius, radius
+
+    chunks = range(CHUNKS)
+    sharp = sharp_ref[0]
+    shift = offset_ref[0]
+
+    txt_unit, _ = unit(caption_ref[...])
+    txt[OWN] = txt_unit.astype(jnp.bfloat16)
+    pl.semaphore_wait(barrier, 4)
+    for c in chunks:
+        send_txt(OWN, Y, c, 0, to_y)
+    img_unit, _ = unit(picture_ref[...])
+    img_high = img_unit.astype(jnp.bfloat16)
+    img[OWN] = img_high
+    for c in chunks:
+        send_img(OWN, X, c, 1, to_x)
+    for c in chunks:
+        send_txt(OWN, SIB, c, 2, to_sib)
+        send_img(OWN, SIB, c, 3, to_sib)
+    img_low[...] = (img_unit - img_high.astype(jnp.float32)).astype(jnp.bfloat16)
+
+    loss_ref[...] = jnp.zeros_like(loss_ref)
+    grad_image_ref[...] = jnp.zeros_like(grad_image_ref)
+    grad_text_ref[...] = jnp.zeros_like(grad_text_ref)
+
+    def product(a, b):
+        return lax.dot_general(a, b, (((1,), (1,)), ((), ())), preferred_element_type=jnp.float32)
+
+    def gather(coeff, block, acc):
+        high = coeff.astype(jnp.bfloat16)
+        low = (coeff - high.astype(jnp.float32)).astype(jnp.bfloat16)
+        acc[...] += jnp.dot(high, block, preferred_element_type=jnp.float32) + jnp.dot(
+            low, block, preferred_element_type=jnp.float32
+        )
+
+    def diagonal():
+        shape = (rows, rows)
+        return lax.broadcasted_iota(jnp.int32, shape, 0) == lax.broadcasted_iota(jnp.int32, shape, 1)
+
+    def image_side(slot, diag=False):
+        block = txt[slot]
+        z = sharp * (product(img[OWN], block) + product(img_low[...], block)) + shift
+        e = jnp.exp(-jnp.abs(z))
+        loss = jnp.maximum(z, 0.0) + jnp.log1p(e)
+        coeff = jnp.where(z >= 0, 1.0, e) / (1.0 + e)
+        if diag:
+            loss = loss - jnp.where(diagonal(), z, 0.0)
+            coeff = coeff - jnp.where(diagonal(), 1.0, 0.0)
+        loss_ref[...] += jnp.sum(loss, axis=1, keepdims=True)
+        gather(coeff, block, grad_image_ref)
+
+    def text_side(slot, diag=False):
+        block = img[slot]
+        z = sharp * product(txt[OWN], block) + shift
+        e = jnp.exp(-jnp.abs(z))
+        coeff = jnp.where(z >= 0, 1.0, e) / (1.0 + e)
+        if diag:
+            coeff = coeff - jnp.where(diagonal(), 1.0, 0.0)
+        gather(coeff, block, grad_text_ref)
+
+    image_side(OWN, True)
+    text_side(OWN, True)
+
+    for c in chunks:
+        wait_txt(Y, c)
+        @pl.when(jnp.logical_not(skip_txt_z))
+        def _():
+            send_txt(Y, Z, c, 4, z_out)
+        wait_img(X, c)
+        send_img(X, V, c, 5, to_y)
+        send_img(X, SIB_X, c, 6, to_sib)
+        send_img(OWN, Y, c, 7, to_y)
+        send_txt(OWN, X, c, 8, to_x)
+
+    for c in chunks:
+        wait_txt(SIB, c)
+        wait_img(SIB, c)
+    image_side(SIB)
+    text_side(SIB)
+    text_side(X)
+
+    early = lax.rem(y + core, 2) == 0
+    for c in chunks:
+        @pl.when(corner)
+        def _():
+            send_txt(Y, FAR, c, 9, to_x)
+        @pl.when(jnp.logical_not(skip_txt_z))
+        def _():
+            wait_txt(Z, c)
+        @pl.when(jnp.logical_not(corner))
+        def _():
+            send_txt(Z, FAR, c, 9, to_x)
+        send_txt(lax.select(early, Y, Z), SIB_E, c, 10, to_sib)
+        wait_img(V, c)
+        @pl.when(corner)
+        def _():
+            send_img(V, FAR, c, 11, z_out)
+        wait_img(Y, c)
+        @pl.when(jnp.logical_not(skip_img_z))
+        def _():
+            send_img(Y, Z, c, 12, z_out)
+        wait_txt(X, c)
+        send_txt(X, SIB_X, c, 13, to_sib)
+
+    for c in chunks:
+        wait_img(SIB_X, c)
+    text_side(SIB_X)
+    image_side(X)
+    image_side(lax.select(y == 0, Z, Y))
+    for c in chunks:
+        wait_txt(SIB_E, c)
+        wait_txt(SIB_X, c)
+    image_side(SIB_E)
+    image_side(SIB_X)
+
+    for c in chunks:
+        @pl.when(jnp.logical_not(skip_img_z))
+        def _():
+            wait_img(Z, c)
+        send_img(lax.select(early, Y, Z), SIB_E, c, 14, to_sib)
+        wait_txt(FAR, c)
+        send_txt(FAR, SIB_F, c, 15, to_sib)
+        @pl.when(corner)
+        def _():
+            wait_img(FAR, c)
+        send_img(lax.select(corner, FAR, V), SIB_F, c, 16, to_sib)
+    text_side(lax.select(y == 0, Y, Z))
+    image_side(FAR)
+    text_side(lax.select(corner, FAR, V))
+    for c in chunks:
+        wait_img(SIB_E, c)
+        wait_txt(SIB_F, c)
+        wait_img(SIB_F, c)
+    text_side(SIB_E)
+    image_side(SIB_F)
+    text_side(SIB_F)
+
+    def back(raw, acc):
+        own, radius = unit(raw)
+        grad = sharp * acc
+        inner = jnp.sum(own * grad, axis=-1, keepdims=True)
+        return (grad - own * inner) / radius
+
+    loss_ref[...] = loss_ref[...] * (1.0 / (STEPS * rows))
+    grad_image_ref[...] = back(picture_ref[...], grad_image_ref[...])
+    grad_text_ref[...] = back(caption_ref[...], grad_text_ref[...])
+
+    def sent(number):
+        for c in chunks:
+            copy(txt, txt_sem, OWN, OWN, c, number, to_sib).wait_send()
+
+    for number in (0, 1, 2, 3, 5, 6, 7, 8, 9, 10, 13, 14, 15, 16):
+        sent(number)
+
+    @pl.when(jnp.logical_not(skip_txt_z))
+    def _():
+        sent(4)
+
+    @pl.when(corner)
+    def _():
+        sent(11)
+
+    @pl.when(jnp.logical_not(skip_img_z))
+    def _():
+        sent(12)
+
+
+def per_device_tree(picture, caption, sharpness, offset):
+    rows, width = picture.shape
+    vmem = pl.BlockSpec(memory_space=pltpu.VMEM)
+    smem = pl.BlockSpec(memory_space=pltpu.SMEM)
+    loss, grad_image, grad_text = pl.pallas_call(
+        tree_kernel,
+        out_shape=(
+            jax.ShapeDtypeStruct((rows, 1), jnp.float32),
+            jax.ShapeDtypeStruct((rows, width), jnp.float32),
+            jax.ShapeDtypeStruct((rows, width), jnp.float32),
+        ),
+        in_specs=[vmem, vmem, smem, smem],
+        out_specs=(vmem, vmem, vmem),
+        scratch_shapes=[
+            pltpu.VMEM((SLOTS, rows, width), jnp.bfloat16),
+            pltpu.VMEM((SLOTS, rows, width), jnp.bfloat16),
+            pltpu.VMEM((rows, width), jnp.bfloat16),
+            pltpu.SemaphoreType.DMA((SLOTS, CHUNKS)),
+            pltpu.SemaphoreType.DMA((SLOTS, CHUNKS)),
+            pltpu.SemaphoreType.DMA((SENDS, CHUNKS)),
+        ],
+        compiler_params=pltpu.CompilerParams(
+            collective_id=0, has_side_effects=True, vmem_limit_bytes=48 * 1024 * 1024
+        ),
+        cost_estimate=pl.CostEstimate(
+            flops=14 * STEPS * rows * rows * width,
+            bytes_accessed=16 * rows * width,
+            transcendentals=4 * STEPS * rows * rows,
+        ),
+    )(picture, caption, sharpness, offset)
+    return loss.reshape(rows), grad_image, grad_text
+
+
 def solution(mesh):
+    body = per_device_tree if mesh.shape["dp"] == 32 else per_device
     return jax.shard_map(
-        per_device,
+        body,
         mesh=mesh,
         in_specs=(P("dp", None), P("dp", None), P(), P()),
         out_specs=(P("dp"), P("dp", None), P("dp", None)),

time: 197 us -> 65.4 us (0.33)
  waiting for transfers between devices: 96.7 us -> 0 us
  starting transfers between devices: 64.9 us -> 0 us
  Pallas kernels: 0 us -> 57.5 us
  matrix products: 26.9 us -> 0 us
  other arithmetic: 5.93 us -> 0.68 us
  local copies, waits for them, and re-layouts: 0.08 us -> 4.56 us
    ppermute x16 -> x0, waiting for transfers between devices: 96.7 us -> none  [shifted(): lax.ppermute(value, axis, [(i, (i + by) % size) for i in range(size)])]
    ppermute x16 -> x0, starting transfers between devices: 64.9 us -> none  [shifted(): lax.ppermute(value, axis, [(i, (i + by) % size) for i in range(size)])]
    pallas_call x0 -> x1, Pallas kernels: none -> 57.5 us  [per_device_tree(): pl.pallas_call(tree_kernel, out_shape=(jax.ShapeDtypeStruct((rows, 1), jn...]
    dot_general x24 -> x0, matrix products: 26.9 us -> none  [the longest x8 11.1 us: per_device(): jnp.dot(match_weight_factor.T, image_unit_vectors, precision=lax.Precisio...]
    unnamed x4 -> x6, local copies, waits for them, and re-layouts: 0.08 us -> 4.56 us
    div x3 -> x0, other arithmetic: 3.1 us -> none  [the longest x2 2.52 us: back_rows(): return (grad_unit - unit * inner) / radius]
  transfers between devices with their start and end apart: 16 -> 0, of which waited for: 11 -> 0; matrix products, arithmetic and copies ran while one was open for 14% -> 0% of each run, Pallas kernels for 0% -> 0%
where the time goes in v1:
time: 65.4 us; the launch traced here: 64.7 us
  Pallas kernels  57.5 us (88%)
  local copies, waits for them, and re-layouts  4.56 us (7%)
  between operations  1.94 us (3%)
  other arithmetic  0.68 us (1%)
    pallas_call x1, Pallas kernels, per_device_tree(): pl.pallas_call(tree_kernel, out_shape=(jax.ShapeDtypeStruct((rows, 1), jn...  57.5 us
    unnamed x6, local copies, waits for them, and re-layouts  4.56 us

profile of v1, /device:TPU:0, one launch (start us, length us, event | category | flops | bytes accessed | tf_op | source)
XLA Modules:
  0.0 64.7 jit_solution(13694609463606069756)
XLA Ops:
  1.9 0.0 copy-start
  1.9 1.3 %copy-done = f32[256,1152]{1,0:T(8,128)S(1)} copy-done((f32[256,1152]{1,0:T(8,128)S(1)}, f32[256,1152]{1,0:T(8,128)}, u32[]{:S(2)}) %copy-start) | copy-done | bytes 1179672
  3.2 0.0 copy-start.1
  3.2 1.3 %copy-done.1 = f32[256,1152]{1,0:T(8,128)S(1)} copy-done((f32[256,1152]{1,0:T(8,128)S(1)}, f32[256,1152]{1,0:T(8,128)}, u32[]{:S(2)}) %copy-start.1) | copy-done | bytes 1179672
  4.5 57.5 %shard_map.67 = (f32[256,1]{1,0:T(8,128)S(1)}, f32[256,1152]{1,0:T(8,128)S(1)}, f32[256,1152]{1,0:T(8,128)S(1)}) custom-call(f32[256,1152]{1,0:T(8,128)S(1)} %copy-done, f32[256,1152]{1,0:T(8,128)S(1)} %copy-done.1, f32[1]{0:T(128)S(6)} %copy.9.sharp_ref, f32[1]{0:T(128)S(6)} %copy.10.offset_ref), custom_call_target="tpu_custom_call" | custom-call | flops 8455716864 | bytes 4718592 | tf_op jit(solution)/shard_map/pallas_call | solution.py:314
  62.0 0.7 %reduce = f32[256]{0:T(256)} reduce(f32[256,1]{1,0:T(8,128)S(1)} %get-tuple-element.6, f32[]{:T(128)} %constant), dimensions={1}, to_apply=%get-tuple-element.6.reduce_sub_computation | reduce | bytes 2052 | tf_op jit(solution)/shard_map/pallas_call | solution.py:314
  62.7 1.0 %copy.11 = f32[256,1152]{1,0:T(8,128)} copy(f32[256,1152]{1,0:T(8,128)S(1)} %get-tuple-element.13) | data formatting | bytes 2359296
  63.7 1.0 %copy.12 = f32[256,1152]{1,0:T(8,128)} copy(f32[256,1152]{1,0:T(8,128)S(1)} %get-tuple-element.14) | data formatting | bytes 2359296
Async XLA Ops:
  1.9 1.3 %copy-start = (f32[256,1152]{1,0:T(8,128)S(1)}, f32[256,1152]{1,0:T(8,128)}, u32[]{:S(2)}) copy-start(f32[256,1152]{1,0:T(8,128)} %picture_ref.1) | copy-start | bytes 3538948
  3.2 1.3 %copy-start.1 = (f32[256,1152]{1,0:T(8,128)S(1)}, f32[256,1152]{1,0:T(8,128)}, u32[]{:S(2)}) copy-start(f32[256,1152]{1,0:T(8,128)} %caption_ref.1) | copy-start | bytes 3538948

commit v2 on v1

--- a/solution.py
+++ b/solution.py
@@ -157,6 +157,14 @@
     for c in chunks:
         send_img(OWN, X, c, 1, to_x)
     for c in chunks:
+        send_txt(OWN, X, c, 8, to_x)
+
+    @pl.when(corner)
+    def _():
+        for c in chunks:
+            send_img(OWN, Y, c, 7, to_y)
+
+    for c in chunks:
         send_txt(OWN, SIB, c, 2, to_sib)
         send_img(OWN, SIB, c, 3, to_sib)
     img_low[...] = (img_unit - img_high.astype(jnp.float32)).astype(jnp.bfloat16)
@@ -200,19 +208,48 @@
             coeff = coeff - jnp.where(diagonal(), 1.0, 0.0)
         gather(coeff, block, grad_text_ref)
 
+    def back(raw, acc):
+        own, radius = unit(raw)
+        grad = sharp * acc
+        inner = jnp.sum(own * grad, axis=-1, keepdims=True)
+        return (grad - own * inner) / radius
+
+    def image_back():
+        loss_ref[...] = loss_ref[...] * (1.0 / (STEPS * rows))
+        grad_image_ref[...] = back(picture_ref[...], grad_image_ref[...])
+
+    inner = jnp.logical_not(corner)
+    early = lax.rem(y + core, 2) == 0
+    late = jnp.logical_not(early)
+
     image_side(OWN, True)
     text_side(OWN, True)
 
     for c in chunks:
         wait_txt(Y, c)
+
         @pl.when(jnp.logical_not(skip_txt_z))
         def _():
             send_txt(Y, Z, c, 4, z_out)
+
         wait_img(X, c)
         send_img(X, V, c, 5, to_y)
         send_img(X, SIB_X, c, 6, to_sib)
-        send_img(OWN, Y, c, 7, to_y)
-        send_txt(OWN, X, c, 8, to_x)
+
+    @pl.when(inner)
+    def _():
+        for c in chunks:
+            send_img(OWN, Y, c, 7, to_y)
+
+    @pl.when(corner)
+    def _():
+        for c in chunks:
+            send_txt(Y, FAR, c, 9, to_x)
+
+    @pl.when(early)
+    def _():
+        for c in chunks:
+            send_txt(Y, SIB_E, c, 10, to_sib)
 
     for c in chunks:
         wait_txt(SIB, c)
@@ -221,26 +258,32 @@
     text_side(SIB)
     text_side(X)
 
-    early = lax.rem(y + core, 2) == 0
-    for c in chunks:
+    for c in chunks:
+        @pl.when(jnp.logical_not(skip_txt_z))
+        def _():
+            wait_txt(Z, c)
+
+        @pl.when(inner)
+        def _():
+            send_txt(Z, FAR, c, 9, to_x)
+
+        @pl.when(late)
+        def _():
+            send_txt(Z, SIB_E, c, 10, to_sib)
+
         @pl.when(corner)
         def _():
-            send_txt(Y, FAR, c, 9, to_x)
-        @pl.when(jnp.logical_not(skip_txt_z))
-        def _():
-            wait_txt(Z, c)
-        @pl.when(jnp.logical_not(corner))
-        def _():
-            send_txt(Z, FAR, c, 9, to_x)
-        send_txt(lax.select(early, Y, Z), SIB_E, c, 10, to_sib)
-        wait_img(V, c)
-        @pl.when(corner)
-        def _():
+            wait_img(V, c)
             send_img(V, FAR, c, 11, z_out)
-        wait_img(Y, c)
-        @pl.when(jnp.logical_not(skip_img_z))
-        def _():
-            send_img(Y, Z, c, 12, z_out)
+
+        @pl.when(inner)
+        def _():
+            wait_img(Y, c)
+
+            @pl.when(jnp.logical_not(skip_img_z))
+            def _():
+                send_img(Y, Z, c, 12, z_out)
+
         wait_txt(X, c)
         send_txt(X, SIB_X, c, 13, to_sib)
 
@@ -256,35 +299,52 @@
     image_side(SIB_X)
 
     for c in chunks:
-        @pl.when(jnp.logical_not(skip_img_z))
-        def _():
-            wait_img(Z, c)
-        send_img(lax.select(early, Y, Z), SIB_E, c, 14, to_sib)
+        @pl.when(corner)
+        def _():
+            wait_img(Y, c)
+
+            @pl.when(jnp.logical_not(skip_img_z))
+            def _():
+                send_img(Y, Z, c, 12, z_out)
+
+            wait_img(FAR, c)
+            send_img(FAR, SIB_F, c, 16, to_sib)
+
+        @pl.when(inner)
+        def _():
+            wait_img(V, c)
+            send_img(V, SIB_F, c, 16, to_sib)
+
         wait_txt(FAR, c)
         send_txt(FAR, SIB_F, c, 15, to_sib)
-        @pl.when(corner)
-        def _():
-            wait_img(FAR, c)
-        send_img(lax.select(corner, FAR, V), SIB_F, c, 16, to_sib)
-    text_side(lax.select(y == 0, Y, Z))
+
+    @pl.when(early)
+    def _():
+        for c in chunks:
+            send_img(Y, SIB_E, c, 14, to_sib)
+
+    text_side(lax.select(corner, FAR, V))
     image_side(FAR)
-    text_side(lax.select(corner, FAR, V))
-    for c in chunks:
-        wait_img(SIB_E, c)
+    for c in chunks:
         wait_txt(SIB_F, c)
         wait_img(SIB_F, c)
-    text_side(SIB_E)
     image_side(SIB_F)
     text_side(SIB_F)
-
-    def back(raw, acc):
-        own, radius = unit(raw)
-        grad = sharp * acc
-        inner = jnp.sum(own * grad, axis=-1, keepdims=True)
-        return (grad - own * inner) / radius
-
-    loss_ref[...] = loss_ref[...] * (1.0 / (STEPS * rows))
-    grad_image_ref[...] = back(picture_ref[...], grad_image_ref[...])
+    image_back()
+
+    for c in chunks:
+        @pl.when(jnp.logical_not(skip_img_z))
+        def _():
+            wait_img(Z, c)
+
+        @pl.when(late)
+        def _():
+            send_img(Z, SIB_E, c, 14, to_sib)
+
+    text_side(lax.select(y == 0, Y, Z))
+    for c in chunks:
+        wait_img(SIB_E, c)
+    text_side(SIB_E)
     grad_text_ref[...] = back(caption_ref[...], grad_text_ref[...])
 
     def sent(number):

time: 65.4 us -> 60.5 us (0.925)
  Pallas kernels: 57.5 us -> 52.8 us
    pallas_call x1, Pallas kernels: 57.5 us -> 52.8 us  [per_device_tree(): pl.pallas_call(tree_kernel, out_shape=(jax.ShapeDtypeStruct((rows, 1), jn...]
where the time goes in v2:
time: 60.5 us; the launch traced here: 60 us
  Pallas kernels  52.8 us (87%)
  local copies, waits for them, and re-layouts  4.56 us (8%)
  between operations  1.94 us (3%)
  other arithmetic  0.68 us (1%)
    pallas_call x1, Pallas kernels, per_device_tree(): pl.pallas_call(tree_kernel, out_shape=(jax.ShapeDtypeStruct((rows, 1), jn...  52.8 us
    unnamed x6, local copies, waits for them, and re-layouts  4.56 us

profile of v2, /device:TPU:0, one launch (start us, length us, event | category | flops | bytes accessed | tf_op | source)
XLA Modules:
  0.0 60.0 jit_solution(5340707847330409537)
XLA Ops:
  1.9 0.0 copy-start
  1.9 1.3 %copy-done = f32[256,1152]{1,0:T(8,128)S(1)} copy-done((f32[256,1152]{1,0:T(8,128)S(1)}, f32[256,1152]{1,0:T(8,128)}, u32[]{:S(2)}) %copy-start) | copy-done | bytes 1179672
  3.2 0.0 copy-start.1
  3.2 1.3 %copy-done.1 = f32[256,1152]{1,0:T(8,128)S(1)} copy-done((f32[256,1152]{1,0:T(8,128)S(1)}, f32[256,1152]{1,0:T(8,128)}, u32[]{:S(2)}) %copy-start.1) | copy-done | bytes 1179672
  4.5 52.8 %shard_map.67 = (f32[256,1]{1,0:T(8,128)S(1)}, f32[256,1152]{1,0:T(8,128)S(1)}, f32[256,1152]{1,0:T(8,128)S(1)}) custom-call(f32[256,1152]{1,0:T(8,128)S(1)} %copy-done, f32[256,1152]{1,0:T(8,128)S(1)} %copy-done.1, f32[1]{0:T(128)S(6)} %copy.9.sharp_ref, f32[1]{0:T(128)S(6)} %copy.10.offset_ref), custom_call_target="tpu_custom_call" | custom-call | flops 8455716864 | bytes 4718592 | tf_op jit(solution)/shard_map/pallas_call | solution.py:374
  57.3 0.7 %reduce = f32[256]{0:T(256)} reduce(f32[256,1]{1,0:T(8,128)S(1)} %get-tuple-element.6, f32[]{:T(128)} %constant), dimensions={1}, to_apply=%get-tuple-element.6.reduce_sub_computation | reduce | bytes 2052 | tf_op jit(solution)/shard_map/pallas_call | solution.py:374
  58.0 1.0 %copy.11 = f32[256,1152]{1,0:T(8,128)} copy(f32[256,1152]{1,0:T(8,128)S(1)} %get-tuple-element.13) | data formatting | bytes 2359296
  59.0 1.0 %copy.12 = f32[256,1152]{1,0:T(8,128)} copy(f32[256,1152]{1,0:T(8,128)S(1)} %get-tuple-element.14) | data formatting | bytes 2359296
Async XLA Ops:
  1.9 1.3 %copy-start = (f32[256,1152]{1,0:T(8,128)S(1)}, f32[256,1152]{1,0:T(8,128)}, u32[]{:S(2)}) copy-start(f32[256,1152]{1,0:T(8,128)} %picture_ref.1) | copy-start | bytes 3538948
  3.2 1.3 %copy-start.1 = (f32[256,1152]{1,0:T(8,128)S(1)}, f32[256,1152]{1,0:T(8,128)}, u32[]{:S(2)}) copy-start(f32[256,1152]{1,0:T(8,128)} %caption_ref.1) | copy-start | bytes 3538948

commit v3 on v2

--- a/solution.py
+++ b/solution.py
@@ -146,16 +146,18 @@
     sharp = sharp_ref[0]
     shift = offset_ref[0]
 
-    txt_unit, _ = unit(caption_ref[...])
-    txt[OWN] = txt_unit.astype(jnp.bfloat16)
-    pl.semaphore_wait(barrier, 4)
-    for c in chunks:
+    for c in chunks:
+        at = pl.ds(c * part, part)
+        txt[OWN, at] = unit(caption_ref[at])[0].astype(jnp.bfloat16)
+        if c == 0:
+            pl.semaphore_wait(barrier, 4)
         send_txt(OWN, Y, c, 0, to_y)
-    img_unit, _ = unit(picture_ref[...])
-    img_high = img_unit.astype(jnp.bfloat16)
-    img[OWN] = img_high
-    for c in chunks:
+        img_unit = unit(picture_ref[at])[0]
+        img_high = img_unit.astype(jnp.bfloat16)
+        img[OWN, at] = img_high
         send_img(OWN, X, c, 1, to_x)
+        img_low[at] = (img_unit - img_high.astype(jnp.float32)).astype(jnp.bfloat16)
+
     for c in chunks:
         send_txt(OWN, X, c, 8, to_x)
 
@@ -167,7 +169,6 @@
     for c in chunks:
         send_txt(OWN, SIB, c, 2, to_sib)
         send_img(OWN, SIB, c, 3, to_sib)
-    img_low[...] = (img_unit - img_high.astype(jnp.float32)).astype(jnp.bfloat16)
 
     loss_ref[...] = jnp.zeros_like(loss_ref)
     grad_image_ref[...] = jnp.zeros_like(grad_image_ref)
@@ -197,7 +198,7 @@
             loss = loss - jnp.where(diagonal(), z, 0.0)
             coeff = coeff - jnp.where(diagonal(), 1.0, 0.0)
         loss_ref[...] += jnp.sum(loss, axis=1, keepdims=True)
-        gather(coeff, block, grad_image_ref)
+        grad_image_ref[...] += jnp.dot(coeff.astype(jnp.bfloat16), block, preferred_element_type=jnp.float32)
 
     def text_side(slot, diag=False):
         block = img[slot]

time: 60.5 us -> 60.2 us (level)
  no operation moved by 1% of the time
where the time goes in v3:
time: 60.2 us; the launch traced here: 59.9 us
  Pallas kernels  52.7 us (88%)
  local copies, waits for them, and re-layouts  4.56 us (8%)
  between operations  1.94 us (3%)
  other arithmetic  0.68 us (1%)
    pallas_call x1, Pallas kernels, per_device_tree(): pl.pallas_call(tree_kernel, out_shape=(jax.ShapeDtypeStruct((rows, 1), jn...  52.7 us
    unnamed x6, local copies, waits for them, and re-layouts  4.56 us

profile of v3, /device:TPU:0, one launch (start us, length us, event | category | flops | bytes accessed | tf_op | source)
XLA Modules:
  0.0 59.9 jit_solution(16292568136587379635)
XLA Ops:
  1.9 0.0 copy-start
  1.9 1.3 %copy-done = f32[256,1152]{1,0:T(8,128)S(1)} copy-done((f32[256,1152]{1,0:T(8,128)S(1)}, f32[256,1152]{1,0:T(8,128)}, u32[]{:S(2)}) %copy-start) | copy-done | bytes 1179672
  3.2 0.0 copy-start.1
  3.2 1.3 %copy-done.1 = f32[256,1152]{1,0:T(8,128)S(1)} copy-done((f32[256,1152]{1,0:T(8,128)S(1)}, f32[256,1152]{1,0:T(8,128)}, u32[]{:S(2)}) %copy-start.1) | copy-done | bytes 1179672
  4.5 52.7 %shard_map.67 = (f32[256,1]{1,0:T(8,128)S(1)}, f32[256,1152]{1,0:T(8,128)S(1)}, f32[256,1152]{1,0:T(8,128)S(1)}) custom-call(f32[256,1152]{1,0:T(8,128)S(1)} %copy-done, f32[256,1152]{1,0:T(8,128)S(1)} %copy-done.1, f32[1]{0:T(128)S(6)} %copy.9.sharp_ref, f32[1]{0:T(128)S(6)} %copy.10.offset_ref), custom_call_target="tpu_custom_call" | custom-call | flops 8455716864 | bytes 4718592 | tf_op jit(solution)/shard_map/pallas_call | solution.py:375
  57.1 0.7 %reduce = f32[256]{0:T(256)} reduce(f32[256,1]{1,0:T(8,128)S(1)} %get-tuple-element.6, f32[]{:T(128)} %constant), dimensions={1}, to_apply=%get-tuple-element.6.reduce_sub_computation | reduce | bytes 2052 | tf_op jit(solution)/shard_map/pallas_call | solution.py:375
  57.8 1.0 %copy.11 = f32[256,1152]{1,0:T(8,128)} copy(f32[256,1152]{1,0:T(8,128)S(1)} %get-tuple-element.13) | data formatting | bytes 2359296
  58.8 1.0 %copy.12 = f32[256,1152]{1,0:T(8,128)} copy(f32[256,1152]{1,0:T(8,128)S(1)} %get-tuple-element.14) | data formatting | bytes 2359296
Async XLA Ops:
  1.9 1.3 %copy-start = (f32[256,1152]{1,0:T(8,128)S(1)}, f32[256,1152]{1,0:T(8,128)}, u32[]{:S(2)}) copy-start(f32[256,1152]{1,0:T(8,128)} %picture_ref.1) | copy-start | bytes 3538948
  3.2 1.3 %copy-start.1 = (f32[256,1152]{1,0:T(8,128)S(1)}, f32[256,1152]{1,0:T(8,128)}, u32[]{:S(2)}) copy-start(f32[256,1152]{1,0:T(8,128)} %caption_ref.1) | copy-start | bytes 3538948
